TPU v7x, 32 devices: a whole 2x2x4 slice. The times are simulated.
32 devices in a mesh: tok: 8 (over z, x), head: 4 (over y, core).
Axes of the slice: x: 2, y: 2, z: 4, core: 2. Of those that a mesh axis runs over, the one named last changes fastest.
Arguments:
- tokens: bfloat16 [4096, 1664], P(('tok', 'head')), may hold values from -75 to 75
- attn_gain: float32 [1664], replicated, may hold values from 0.1 to 1.9
- qkv_weight: bfloat16 [3, 1664, 1664], P(None, 'head'), may hold values from -5 to 5
- out_weight: bfloat16 [1664, 1664], P('head'), may hold values from -0.4375 to 0.4375
- merge_gain: float32 [1664], replicated, may hold values from 0.1 to 1.9
- merge_weight: bfloat16 [6656, 4096], P('head', 'tok'), may hold values from -0.078125 to 0.078125
- grid_sizes: int32 [2, 16], P(None, 'tok'), may hold values from 2 to 16, as said below
- segment_ids: int32 [4096], P('tok'), may hold values from 0 to 15, as said below
- patch_pos: int32 [2, 4096], P(None, 'tok'), may hold values from 0 to 15, as said below
- live_mask: int32 [4096], P('tok'), may hold values from 0 to 1, as said below
- owners: int32 [1024, 1], P(('tok', 'head')), may hold values from 0 to 7; in each aligned block of 32 rows (0 to 31, 32 to 63, ...) at most 8 rows name the same one
Outputs:
- delivered: bfloat16 [2048, 4096], P(('tok', 'head'))
Inputs may be any that keep to these rules, and one draw needn't show every extreme that they name: `grid_sizes`: both sides of every image are even, and some image is 16 by 16. `segment_ids`: never fall along the tokens. The aligned block b of 512 tokens holds images b * 2 to (b + 1) * 2 - 1 packed in order from the block's start, image s taking grid_sizes[0, s] * grid_sizes[1, s] tokens; the block's remaining tokens carry the number of its last image. `patch_pos`: an image's tokens come in 2x2 windows, windows in row-major order, each window as (2 * r, 2 * c), (2 * r, 2 * c + 1), (2 * r + 1, 2 * c), (2 * r + 1, 2 * c + 1); padding tokens sit at (0, 0). `live_mask`: 1 exactly on the tokens that belong to an image. `owners`: in each aligned block of 32 rows (the merged rows of one device) no owner is named more than 8 times.
All inputs are finite; a program needn't handle non-finite values.
Results may differ from a plain program's by a relative error of at most 0.024.
Values may be sent and summed in bfloat16 or wider, within the bound.
A program may use at most 64 MiB of HBM per device.

v0:
```python
import jax
import jax.numpy as jnp
from jax import lax
from jax.sharding import PartitionSpec as P

D = 1664
HD = 104
SIDE = 16


EPSILON = 1e-06
NEGATIVE = -1e30


def layer_norm(values, gain_vec):
    average = jnp.mean(values, axis=-1, keepdims=True)
    centred = values - average
    variance = jnp.mean(centred * centred, axis=-1, keepdims=True)
    return centred * lax.rsqrt(variance + EPSILON) * gain_vec


def rotate(vectors, row_coord, col_coord):
    quarter = vectors.shape[-1] // 4
    frequency = 10000.0 ** (-jnp.arange(quarter, dtype=jnp.float32) / quarter)
    pieces = []
    for which_axis, coordinate in ((0, row_coord), (1, col_coord)):
        leading = vectors[..., 2 * which_axis * quarter : (2 * which_axis + 1) * quarter]
        trailing = vectors[..., (2 * which_axis + 1) * quarter : (2 * which_axis + 2) * quarter]
        angles = coordinate[:, None, None] * frequency
        cosine = jnp.cos(angles)
        sine_val = jnp.sin(angles)
        pieces.append(leading * cosine - trailing * sine_val)
        pieces.append(leading * sine_val + trailing * cosine)
    return jnp.concatenate(pieces, axis=-1)


def body(
    tokens,
    attn_gain,
    qkv_weight,
    out_weight,
    merge_gain,
    merge_weight,
    grid_sizes,
    segment_ids,
    patch_pos,
    live_mask,
    owners,
):
    group_len = segment_ids.shape[0]
    local_rows = tokens.shape[0]
    head_width = qkv_weight.shape[1]
    heads_here = head_width // HD
    tok_count = lax.axis_size("tok")
    image_count = grid_sizes.shape[1]
    local_image = segment_ids - lax.axis_index("tok") * image_count
    image_match = local_image[:, None] == jnp.arange(image_count, dtype=jnp.int32)[None, :]
    grid_float = grid_sizes.astype(jnp.float32)
    row_size = jnp.sum(jnp.where(image_match, grid_float[0][None, :], 0.0), axis=1)
    col_size = jnp.sum(jnp.where(image_match, grid_float[1][None, :], 0.0), axis=1)
    row_coord = patch_pos[0].astype(jnp.float32) * SIDE / row_size
    col_coord = patch_pos[1].astype(jnp.float32) * SIDE / col_size
    stacked_weight = qkv_weight.reshape(3 * head_width, D)
    normed = layer_norm(tokens.astype(jnp.float32), attn_gain).astype(jnp.bfloat16)
    projected_rows = lax.dot_general(
        lax.all_gather(normed, "head", axis=0, tiled=True),
        stacked_weight,
        (((1,), (1,)), ((), ())),
        preferred_element_type=jnp.float32,
    )
    projected_rows = projected_rows.reshape(group_len, 3, heads_here, HD)
    query_all = (rotate(projected_rows[:, 0], row_coord, col_coord) * HD ** (-0.5)).astype(
        jnp.bfloat16
    )
    key_all = rotate(projected_rows[:, 1], row_coord, col_coord).astype(jnp.bfloat16)
    value_all = projected_rows[:, 2].astype(jnp.bfloat16)
    block_len = min(512, group_len)
    block_count = group_len // block_len
    key_live = live_mask == 1

    def allowed_pairs(query_start, span):
        query_seg = lax.dynamic_slice_in_dim(segment_ids, query_start, block_len)
        query_place = query_start + jnp.arange(block_len, dtype=jnp.int32)
        key_place = jnp.arange(span, dtype=jnp.int32)
        same_image = query_seg[:, None] == segment_ids[None, :]
        return same_image & (key_live[None, :] | (query_place[:, None] == key_place[None, :]))

    def query_block(query_start):
        queries = lax.dynamic_slice_in_dim(query_all, query_start, block_len, 0)
        allowed = allowed_pairs(query_start, group_len)
        scores = jnp.einsum("qhd,khd->hqk", queries, key_all, preferred_element_type=jnp.float32)
        masked = jnp.where(allowed[None], scores, NEGATIVE)
        row_top = jnp.max(masked, axis=2, keepdims=True)
        exponent = jnp.where(allowed[None], jnp.exp(masked - row_top), 0.0)
        denominator = jnp.sum(exponent, axis=2)
        numerator = jnp.einsum(
            "hqk,khd->qhd",
            exponent.astype(jnp.bfloat16),
            value_all,
            preferred_element_type=jnp.float32,
        )
        return (numerator / denominator.T[:, :, None]).astype(jnp.bfloat16)

    block_starts = jnp.arange(block_count, dtype=jnp.int32) * block_len
    heads_out = lax.map(query_block, block_starts).reshape(group_len, head_width)
    attn_rows = lax.psum_scatter(
        jnp.dot(heads_out, out_weight, preferred_element_type=jnp.float32).astype(jnp.bfloat16),
        "head",
        scatter_dimension=0,
        tiled=True,
    ).astype(jnp.float32)
    stream = (tokens.astype(jnp.float32) + attn_rows).reshape(local_rows // 4, 4, D)
    average = jnp.sum(stream, axis=2, keepdims=True) / D
    variance = jnp.sum(stream * stream, axis=2, keepdims=True) / D - average * average
    window_rows = ((stream - average) * lax.rsqrt(variance + EPSILON) * merge_gain).astype(
        jnp.bfloat16
    )
    merged_slice = lax.all_to_all(
        window_rows.reshape(local_rows // 4, 4 * D), "head", split_axis=1, concat_axis=0, tiled=True
    )
    merged_count = local_rows // 4
    column_terms = jnp.dot(
        merged_slice,
        lax.all_gather(merge_weight, "tok", axis=1, tiled=True),
        preferred_element_type=jnp.float32,
    )
    projected = lax.psum_scatter(
        column_terms.astype(jnp.bfloat16), "head", scatter_dimension=0, tiled=True
    )
    slot_count = max(2, 2 * merged_count // tok_count)
    owner_col = owners[:, 0]
    owner_hot = (owner_col[:, None] == jnp.arange(tok_count, dtype=jnp.int32)[None, :]).astype(
        jnp.int32
    )
    earlier = jnp.cumsum(owner_hot, axis=0, dtype=jnp.int32) - owner_hot
    slot_index = jnp.sum(earlier * owner_hot, axis=1, dtype=jnp.int32)
    target = owner_col * slot_count + slot_index
    select = (
        jnp.arange(tok_count * slot_count, dtype=jnp.int32)[:, None] == target[None, :]
    ).astype(jnp.bfloat16)
    send_rows = jnp.dot(select, projected, preferred_element_type=jnp.float32).astype(jnp.bfloat16)
    send_rows = send_rows.reshape(tok_count, slot_count, -1)
    received = lax.all_to_all(send_rows, "tok", split_axis=0, concat_axis=0, tiled=True)
    return received.reshape(tok_count * slot_count, -1)


def solution(mesh):
    placed = (
        P(("tok", "head"), None),
        P(),
        P(None, "head", None),
        P("head", None),
        P(),
        P("head", "tok"),
        P(None, "tok"),
        P("tok"),
        P(None, "tok"),
        P("tok"),
        P(("tok", "head"), None),
    )
    return jax.shard_map(
        body, mesh=mesh, in_specs=placed, out_specs=P(("tok", "head"), None), check_vma=False
    )
```

profile of v0, /device:TPU:0, one launch (start us, length us, event | category | flops | bytes accessed | tf_op | source)
XLA Modules:
  0.0 298.7 jit_solution(15643202671974918466)
XLA Ops:
  7.4 1.3 convert_reduce_fusion
  8.6 1.3 fusion.24
  9.9 2.1 fusion.26
  12.1 0.7 convert_element_type.68
  12.8 0.7 broadcast_subtract_fusion
  13.5 0.8 convert_multiply_fusion.1
  14.3 0.7 broadcast_compare_fusion
  15.0 1.0 fusion.21
  16.0 0.5 multiply_cosine_fusion.1
  16.6 18.7 %all-gather.3.cloned.1.call-done = bf16[512,1664]{1,0:T(8,128)(2,1)} async-done(((bf16[128,1664]{1,0:T(8,128)(2,1)}), bf16[512,1664]{1,0:T(8,128)(2,1)}) %all-gather.3.cloned.1.call-update) | async-done | bytes 1703952 | tf_op jit(solution)/shard_map/all_gather | solution.py:66
  35.3 5.2 %fusion.9 = f32[512,3,4,104]{0,3,2,1:T(8,128)S(1)} fusion(bf16[3,4,104,1664]{3,2,1,0:T(8,128)(2,1)} %bitcast.48, bf16[512,1664]{1,0:T(8,128)(2,1)} %all-gather.3.cloned.1.call-done), kind=kOutput, calls=%fused_computation.12 | convolution fusion | flops 2126512128 | bytes 8413184 | tf_op jit(solution)/shard_map/dot_general | solution.py:65
  41.0 0.8 fusion.31
  41.8 2.0 fusion.50
  44.3 2.3 convolution_convert_fusion.2
  46.7 0.5 all-gather.5.cloned.1.call-update
  47.3 28.5 %reduce-scatter.3.cloned.1.call-done = bf16[128,1664]{1,0:T(8,128)(2,1)} async-done(((bf16[512,1664]{1,0:T(8,128)(2,1)}), bf16[128,1664]{1,0:T(8,128)(2,1)}) %reduce-scatter.3.cloned.1.call-update) | async-done | bytes 426000 | tf_op jit(solution)/shard_map/reduce_scatter | solution.py:106
  75.8 1.3 fusion.49
  77.9 10.2 %all_to_all.21 = bf16[32,4,1664]{2,0,1:T(8,128)(2,1)S(1)} all-to-all(bf16[32,4,1664]{2,0,1:T(8,128)(2,1)S(1)} %fusion.30), channel_id=1, replica_groups=mesh['tok'=8,'head'=4] {'head'}, dimensions={1} | all-to-all | bytes 851968 | tf_op jit(solution)/shard_map/all_to_all | solution.py:118
  88.0 150.3 %all-gather.5.cloned.1.call-done = bf16[1664,4096]{1,0:T(8,128)(2,1)} async-done(((bf16[1664,512]{1,0:T(8,128)(2,1)}), bf16[1664,4096]{1,0:T(8,128)(2,1)}) %all-gather.5.cloned.1.call-update) | async-done | bytes 13631504 | tf_op jit(solution)/shard_map/all_gather | solution.py:124
  238.3 8.1 %convolution_convert_fusion = bf16[128,4096]{1,0:T(8,128)(2,1)} fusion(bf16[128,1664]{1,0:T(8,128)(2,1)S(1)} %bitcast.42, bf16[1664,4096]{1,0:T(8,128)(2,1)} %all-gather.5.cloned.1.call-done), kind=kOutput, calls=%fused_computation.1 | convolution fusion | flops 1745354752 | bytes 15106048 | tf_op jit(solution)/shard_map/dot_general | solution.py:122
  246.8 22.9 %reduce-scatter.5.cloned.1.call-done = bf16[32,4096]{1,0:T(8,128)(2,1)} async-done(((bf16[128,4096]{1,0:T(8,128)(2,1)}), bf16[32,4096]{1,0:T(8,128)(2,1)}) %reduce-scatter.5.cloned.1.call-update) | async-done | bytes 262160 | tf_op jit(solution)/shard_map/reduce_scatter | solution.py:127
  269.7 1.2 fusion.1
  271.0 19.8 %all_to_all.22 = bf16[8,8,4096]{2,1,0:T(8,128)(2,1)S(1)} all-to-all(bf16[8,8,4096]{2,1,0:T(8,128)(2,1)S(1)} %fusion.1), channel_id=1, replica_groups=mesh['tok'=8,'head'=4] {'tok'}, dimensions={0} | all-to-all | bytes 1048576 | tf_op jit(solution)/shard_map/all_to_all | solution.py:143
  290.8 0.8 copy.31
  (38 shorter events, 2.4 us)
Async XLA Ops:
  7.4 36.9 %copy-start = (bf16[416,1664]{1,0:T(8,128)(2,1)S(1)}, bf16[416,1664]{1,0:T(8,128)(2,1)}, u32[]{:S(2)}) copy-start(bf16[416,1664]{1,0:T(8,128)(2,1)} %param.14) | copy-start | bytes 4153348
  7.4 27.9 %all-gather.3.cloned.1.call-start = ((), (), s32[]{:S(2)}) async-start(), calls=%async_computation.4 | async-start | bytes 2129920 | tf_op jit(solution)/shard_map/all_gather | solution.py:66
  12.0 63.7 %reduce-scatter.3.cloned.1.call-start = ((), (), s32[]{:S(2)}) async-start(), calls=%async_computation.5 | async-start | bytes 2129920 | tf_op jit(solution)/shard_map/reduce_scatter | solution.py:106
  46.6 29.2 %copy-start.1 = (bf16[128,1664]{1,0:T(8,128)(2,1)S(1)}, bf16[128,1664]{1,0:T(8,128)(2,1)}, u32[]{:S(2)}) copy-start(bf16[128,1664]{1,0:T(8,128)(2,1)} %param.11) | copy-start | bytes 1277956
  46.6 31.1 %copy-start.2 = (f32[1664]{0:T(1024)S(1)}, f32[1664]{0:T(1024)}, u32[]{:S(2)}) copy-start(f32[1664]{0:T(1024)} %param.15) | copy-start | bytes 19972
  46.6 191.7 %all-gather.5.cloned.1.call-start = ((), (), s32[]{:S(2)}) async-start(), calls=%async_computation.6 | async-start | bytes 15335424 | tf_op jit(solution)/shard_map/all_gather | solution.py:124
  47.2 222.5 %reduce-scatter.5.cloned.1.call-start = ((), (), s32[]{:S(2)}) async-start(), calls=%async_computation.7 | async-start | bytes 1310720 | tf_op jit(solution)/shard_map/reduce_scatter | solution.py:127
  238.3 8.2 %copy-start.3 = (s32[32,1]{0,1:T(1,128)S(1)}, s32[32,1]{0,1:T(1,128)}, u32[]{:S(2)}) copy-start(s32[32,1]{0,1:T(1,128)} %param.21) | copy-start | bytes 388
Sparse Core Ops, SparseCore 0:
  12.1 23.0 all-gather.2
  46.8 28.9 reduce-scatter.2
  246.6 23.0 reduce-scatter.4
Sparse Core Ops, SparseCore 1:
  49.3 188.9 all-gather.4
where the time goes:
time: 299 us
  waiting for transfers between devices  221 us (74%)
  blocking collectives  30 us (10%)
  matrix products  18.2 us (6%)
  between operations  14.7 us (5%)
  other arithmetic  13.2 us (4%)
    all_gather x1, waiting for transfers between devices, body(): lax.all_gather(merge_weight, 'tok', axis=1, tiled=True)  150 us
    reduce_scatter x1, waiting for transfers between devices, body(): lax.psum_scatter(jnp.dot(heads_out, out_weight, preferred_element_type=jn...  28.5 us
    reduce_scatter x1, waiting for transfers between devices, body(): lax.psum_scatter(column_terms.astype(jnp.bfloat16), 'head', scatter_dimen...  22.9 us
    all_to_all x1, blocking collectives, body(): lax.all_to_all(send_rows, 'tok', split_axis=0, concat_axis=0, tiled=True)  19.8 us
    all_gather x1, waiting for transfers between devices, body(): lax.all_gather(normed, 'head', axis=0, tiled=True)  18.7 us
    all_to_all x1, blocking collectives, body(): lax.all_to_all(window_rows.reshape(local_rows // 4, 4 * D), 'head', split...  10.2 us
    dot_general x1, matrix products, body(): jnp.dot(merged_slice, lax.all_gather(merge_weight, 'tok', axis=1, tiled=T...  8.14 us
  transfers between devices with their start and end apart: 4, of which 4 were waited for; matrix products, arithmetic and copies ran while one was open for 2% of the time, Pallas kernels for 0%

commit v1 on v0

--- a/solution.py
+++ b/solution.py
@@ -1,6 +1,8 @@
 import jax
 import jax.numpy as jnp
 from jax import lax
+from jax.experimental import pallas as pl
+from jax.experimental.pallas import tpu as pltpu
 from jax.sharding import PartitionSpec as P
 
 D = 1664
@@ -32,6 +34,12 @@
         pieces.append(leading * cosine - trailing * sine_val)
         pieces.append(leading * sine_val + trailing * cosine)
     return jnp.concatenate(pieces, axis=-1)
+
+
+def earlier_rows(owner_col):
+    places = jnp.arange(owner_col.shape[0], dtype=jnp.int32)
+    same = (owner_col[:, None] == owner_col[None, :]) & (places[None, :] < places[:, None])
+    return jnp.sum(same.astype(jnp.int32), axis=1, dtype=jnp.int32)
 
 
 def body(
@@ -129,11 +137,7 @@
     )
     slot_count = max(2, 2 * merged_count // tok_count)
     owner_col = owners[:, 0]
-    owner_hot = (owner_col[:, None] == jnp.arange(tok_count, dtype=jnp.int32)[None, :]).astype(
-        jnp.int32
-    )
-    earlier = jnp.cumsum(owner_hot, axis=0, dtype=jnp.int32) - owner_hot
-    slot_index = jnp.sum(earlier * owner_hot, axis=1, dtype=jnp.int32)
+    slot_index = earlier_rows(owner_col)
     target = owner_col * slot_count + slot_index
     select = (
         jnp.arange(tok_count * slot_count, dtype=jnp.int32)[:, None] == target[None, :]
@@ -144,7 +148,417 @@
     return received.reshape(tok_count * slot_count, -1)
 
 
+VMEM_SPEC = pl.BlockSpec(memory_space=pltpu.VMEM)
+MESH = pl.DeviceIdType.MESH
+VMEM_LIMIT = 48 * 1024 * 1024
+
+
+def remote(source, target, send, arrive, tok, head):
+    return pltpu.make_async_remote_copy(
+        src_ref=source,
+        dst_ref=target,
+        send_sem=send,
+        recv_sem=arrive,
+        device_id=(tok, head),
+        device_id_type=MESH,
+    )
+
+
+def greet(devices):
+    barrier = pltpu.get_barrier_semaphore()
+    for device in devices:
+        pl.semaphore_signal(barrier, inc=1, device_id=device, device_id_type=MESH)
+    pl.semaphore_wait(barrier, len(devices))
+
+
+def head_partners():
+    tok, head = lax.axis_index("tok"), lax.axis_index("head")
+    sibling = head + 1 - 2 * (head % 2)
+    across = (head + 2) % 4
+    return tok, head, sibling, across
+
+
+def gather_kernel(
+    tokens_ref, gain_ref, normed_ref, residual_ref, raw, own_sems, across_sems, relay_sems
+):
+    tok, head, sibling, across = head_partners()
+    diagonal = (sibling + 2) % 4
+    parts = tokens_ref.shape[0]
+    greet([(tok, sibling), (tok, across)])
+
+    def to_across(r):
+        return remote(
+            tokens_ref.at[r], raw.at[1, r], across_sems.at[0, r], across_sems.at[1, r], tok, across
+        )
+
+    def to_sibling(r):
+        return remote(
+            tokens_ref.at[r], raw.at[0, r], own_sems.at[0, r], own_sems.at[1, r], tok, sibling
+        )
+
+    def relay(r):
+        return remote(
+            raw.at[1, r], raw.at[2, r], relay_sems.at[0, r], relay_sems.at[1, r], tok, sibling
+        )
+
+    def settle(rows, r, source):
+        values = rows.astype(jnp.float32)
+        average = jnp.mean(values, axis=-1, keepdims=True)
+        centred = values - average
+        variance = jnp.mean(centred * centred, axis=-1, keepdims=True)
+        normal = centred * lax.rsqrt(variance + EPSILON) * gain_ref[...]
+        normed_ref[r, source] = normal.astype(jnp.bfloat16)
+
+    for r in range(parts):
+        to_across(r).start()
+    for r in range(parts):
+        to_sibling(r).start()
+
+    @pl.loop(0, parts)
+    def _(r):
+        settle(tokens_ref[r], r, head)
+
+    @pl.loop(0, parts)
+    def _(r):
+        to_sibling(r).wait_recv()
+        settle(raw[0, r], r, sibling)
+
+    @pl.loop(0, parts)
+    def _(r):
+        to_across(r).wait_recv()
+        relay(r).start()
+        settle(raw[1, r], r, across)
+
+    @pl.loop(0, parts)
+    def _(r):
+        relay(r).wait_recv()
+        settle(raw[2, r], r, diagonal)
+
+    residual_ref[head] = tokens_ref[head]
+    residual_ref[sibling] = raw[0, head]
+    residual_ref[across] = raw[1, head]
+    residual_ref[diagonal] = raw[2, head]
+
+    @pl.loop(0, parts)
+    def _(r):
+        to_across(r).wait_send()
+        to_sibling(r).wait_send()
+        relay(r).wait_send()
+
+
+def merge_kernel(
+    part_ref, residual_ref, gain_ref, weight_ref, other_ref, target_ref, out_ref,
+    near_sum, sent_sum, far_sum, rows, terms, near_term, sent_term, far_term, places, messages,
+    sum_near_sems, sum_far_sems, row_x_sems, row_z_sems, row_relay_sems,
+    term_near_sems, term_far_sems, place_sems, out_sems, local_sems,
+):
+    tok, head, sibling, across = head_partners()
+    diagonal = (sibling + 2) % 4
+    toks = lax.axis_size("tok")
+    p, q, x = tok // 4, (tok // 2) % 2, tok % 2
+    beside = tok + 1 - 2 * x
+    over = (tok + 4) % 8
+    corner = (beside + 4) % 8
+    span = near_sum.shape[2]
+    chunks = part_ref.shape[1]
+    owned = near_term.shape[2]
+    half = weight_ref.shape[1]
+    greet(
+        [((tok + step) % toks, head) for step in range(1, toks)] + [(tok, sibling), (tok, across)]
+    )
+
+    def near_copy(c, which):
+        block = (diagonal, sibling)[which]
+        return remote(
+            part_ref.at[block, c], near_sum.at[which, c],
+            sum_near_sems.at[0, which, c], sum_near_sems.at[1, which, c], tok, sibling,
+        )
+
+    def far_copy(c):
+        return remote(
+            sent_sum.at[c], far_sum.at[c], sum_far_sems.at[0, c], sum_far_sems.at[1, c], tok, across
+        )
+
+    for c in range(chunks):
+        near_copy(c, 0).start()
+    for c in range(chunks):
+        near_copy(c, 1).start()
+    place_copies = [
+        remote(
+            target_ref, places.at[k], place_sems.at[0, k], place_sems.at[1, k], device, head
+        )
+        for k, device in enumerate((beside, over, corner))
+    ]
+    for copy in place_copies:
+        copy.start()
+
+    @pl.loop(0, chunks)
+    def _(c):
+        near_copy(c, 0).wait_recv()
+        total = part_ref[across, c].astype(jnp.float32) + near_sum[0, c].astype(jnp.float32)
+        sent_sum[c] = total.astype(jnp.bfloat16)
+        far_copy(c).start()
+
+    def row_x(c):
+        return remote(
+            rows.at[0, c], rows.at[1, c], row_x_sems.at[0, c], row_x_sems.at[1, c], beside, head
+        )
+
+    def row_z(c):
+        return remote(
+            rows.at[0, c], rows.at[2, c], row_z_sems.at[0, c], row_z_sems.at[1, c], over, head
+        )
+
+    def row_relay(c):
+        return remote(
+            rows.at[2, c], rows.at[3, c],
+            row_relay_sems.at[0, c], row_relay_sems.at[1, c], beside, head,
+        )
+
+    width = residual_ref.shape[-1]
+
+    @pl.loop(0, chunks)
+    def _(c):
+        near_copy(c, 1).wait_recv()
+        stream = residual_ref[c].astype(jnp.float32) + part_ref[head, c].astype(jnp.float32)
+        stream = stream + near_sum[1, c].astype(jnp.float32)
+        far_copy(c).wait_recv()
+        stream = stream + far_sum[c].astype(jnp.float32)
+        average = jnp.sum(stream, axis=-1, keepdims=True) / width
+        variance = jnp.sum(stream * stream, axis=-1, keepdims=True) / width - average * average
+        normal = (stream - average) * lax.rsqrt(variance + EPSILON) * gain_ref[...]
+        rows[0, c] = normal.astype(jnp.bfloat16)
+        row_z(c).start()
+        row_x(c).start()
+
+    own_columns = pl.ds(pl.multiple_of(q * half, half), half)
+    other_columns = pl.ds(pl.multiple_of((1 - q) * half, half), half)
+
+    def term_near(k, which):
+        block = (diagonal, sibling)[which]
+        return remote(
+            terms.at[k, block], near_term.at[k, which],
+            term_near_sems.at[0, k, which], term_near_sems.at[1, k, which], tok, sibling,
+        )
+
+    def term_far(k):
+        return remote(
+            sent_term.at[k], far_term.at[k], term_far_sems.at[0, k], term_far_sems.at[1, k],
+            tok, across,
+        )
+
+    def project(k):
+        block = rows[k].reshape(chunks * span, width)
+        for weights, columns in ((weight_ref, own_columns), (other_ref, other_columns)):
+            product = jnp.dot(block, weights[...], preferred_element_type=jnp.float32)
+            product = product.astype(jnp.bfloat16).reshape(4, owned, half)
+            terms[k, :, :, columns] = product
+        term_near(k, 0).start()
+        term_near(k, 1).start()
+
+    def pass_on(k):
+        term_near(k, 0).wait_recv()
+        total = terms[k, across].astype(jnp.float32) + near_term[k, 0].astype(jnp.float32)
+        sent_term[k] = total.astype(jnp.bfloat16)
+        term_far(k).start()
+
+    def projected(k):
+        term_near(k, 1).wait_recv()
+        total = terms[k, head].astype(jnp.float32) + near_term[k, 1].astype(jnp.float32)
+        term_far(k).wait_recv()
+        return (total + far_term[k].astype(jnp.float32)).astype(jnp.bfloat16)
+
+    slots = messages.shape[2]
+
+    def delivery(which, step):
+        owner = (tok + step) % toks
+        group = p if which == 0 else 1 - p
+        return remote(
+            messages.at[which, owner], out_ref.at[group, tok],
+            out_sems.at[0, which, step], out_sems.at[1, which, step], owner, head,
+        )
+
+    def kept(which):
+        group = p if which == 0 else 1 - p
+        return pltpu.make_async_copy(
+            messages.at[which, tok], out_ref.at[group, tok], local_sems.at[which]
+        )
+
+    def deliver(which):
+        lines = lax.broadcasted_iota(jnp.int32, (toks * slots, owned), 0).astype(jnp.float32)
+        sent = jnp.zeros((toks * slots, 2 * half), jnp.float32)
+        for turn in range(2):
+            k = 2 * which + turn
+            aim = target_ref[0:1, 0:owned] if k == 0 else places[k - 1, 0:1, 0:owned]
+            side = x if turn == 0 else 1 - x
+            aim = aim + (side * (slots // 2)).astype(jnp.float32)
+            chosen = jnp.where(lines == aim, 1.0, 0.0).astype(jnp.bfloat16)
+            sent = sent + jnp.dot(chosen, projected(k), preferred_element_type=jnp.float32)
+        messages[which] = sent.astype(jnp.bfloat16).reshape(toks, slots, 2 * half)
+        for step in (4, 5, 3, 6, 2, 7, 1):
+            delivery(which, step).start()
+        kept(which).start()
+
+    project(0)
+    pass_on(0)
+
+    @pl.loop(0, chunks)
+    def _(c):
+        row_x(c).wait_recv()
+
+    project(1)
+    pass_on(1)
+
+    @pl.loop(0, chunks)
+    def _(c):
+        row_z(c).wait_recv()
+        row_relay(c).start()
+
+    project(2)
+    pass_on(2)
+    for copy in place_copies:
+        copy.wait_recv()
+    deliver(0)
+
+    @pl.loop(0, chunks)
+    def _(c):
+        row_relay(c).wait_recv()
+
+    project(3)
+    pass_on(3)
+    deliver(1)
+
+    @pl.loop(0, chunks)
+    def _(c):
+        near_copy(c, 0).wait_send()
+        near_copy(c, 1).wait_send()
+        far_copy(c).wait_send()
+        row_x(c).wait_send()
+        row_z(c).wait_send()
+        row_relay(c).wait_send()
+
+    for copy in place_copies:
+        copy.wait_send()
+    for k in range(4):
+        term_near(k, 0).wait_send()
+        term_near(k, 1).wait_send()
+        term_far(k).wait_send()
+    for which in range(2):
+        kept(which).wait()
+        for step in range(1, 8):
+            delivery(which, step).wait()
+
+
+def block_body(
+    tokens, attn_gain, qkv_weight, out_weight, merge_gain, merge_weight,
+    grid_sizes, segment_ids, patch_pos, live_mask, owners,
+):
+    group_len = segment_ids.shape[0]
+    local_rows, width = tokens.shape
+    head_width = qkv_weight.shape[1]
+    heads_here = head_width // HD
+    tok_count = lax.axis_size("tok")
+    owned = local_rows // 4
+    half = merge_weight.shape[1]
+    slot_count = 2 * owned // tok_count
+    dma, vmem = pltpu.SemaphoreType.DMA, pltpu.VMEM
+
+    other_weight = lax.ppermute(merge_weight, "tok", [(t, t ^ 2) for t in range(tok_count)])
+
+    normed, residual = pl.pallas_call(
+        gather_kernel,
+        out_shape=(
+            jax.ShapeDtypeStruct((4, 4, owned, width), jnp.bfloat16),
+            jax.ShapeDtypeStruct((4, owned, width), jnp.bfloat16),
+        ),
+        in_specs=[VMEM_SPEC] * 2,
+        out_specs=(VMEM_SPEC, VMEM_SPEC),
+        scratch_shapes=[vmem((3, 4, owned, width), jnp.bfloat16)] + [dma((2, 4))] * 3,
+        compiler_params=pltpu.CompilerParams(
+            collective_id=0, has_side_effects=True, vmem_limit_bytes=VMEM_LIMIT
+        ),
+    )(tokens.reshape(owned, 4, width).transpose(1, 0, 2), attn_gain.reshape(1, width))
+
+    def by_place(values):
+        return values.reshape(values.shape[:-1] + (group_len // 4, 4)).swapaxes(-1, -2).reshape(
+            values.shape
+        )
+
+    segments = by_place(segment_ids)
+    key_live = by_place(live_mask) == 1
+    places = by_place(patch_pos).astype(jnp.float32)
+    image_count = grid_sizes.shape[1]
+    local_image = segments - lax.axis_index("tok") * image_count
+    image_match = local_image[:, None] == jnp.arange(image_count, dtype=jnp.int32)[None, :]
+    grid_float = grid_sizes.astype(jnp.float32)
+    row_size = jnp.sum(jnp.where(image_match, grid_float[0][None, :], 0.0), axis=1)
+    col_size = jnp.sum(jnp.where(image_match, grid_float[1][None, :], 0.0), axis=1)
+    row_coord = places[0] * SIDE / row_size
+    col_coord = places[1] * SIDE / col_size
+    projected_rows = lax.dot_general(
+        normed.reshape(group_len, width),
+        qkv_weight.reshape(3 * head_width, width),
+        (((1,), (1,)), ((), ())),
+        preferred_element_type=jnp.float32,
+    ).reshape(group_len, 3, heads_here, HD)
+    queries = (rotate(projected_rows[:, 0], row_coord, col_coord) * HD ** (-0.5)).astype(
+        jnp.bfloat16
+    )
+    keys = rotate(projected_rows[:, 1], row_coord, col_coord).astype(jnp.bfloat16)
+    values = projected_rows[:, 2].astype(jnp.bfloat16)
+    order = jnp.arange(group_len, dtype=jnp.int32)
+    allowed = (segments[:, None] == segments[None, :]) & (
+        key_live[None, :] | (order[:, None] == order[None, :])
+    )
+    scores = jnp.einsum("qhd,khd->hqk", queries, keys, preferred_element_type=jnp.float32)
+    masked = jnp.where(allowed[None], scores, NEGATIVE)
+    row_top = jnp.max(masked, axis=2, keepdims=True)
+    exponent = jnp.where(allowed[None], jnp.exp(masked - row_top), 0.0)
+    denominator = jnp.sum(exponent, axis=2)
+    numerator = jnp.einsum(
+        "hqk,khd->qhd", exponent.astype(jnp.bfloat16), values, preferred_element_type=jnp.float32
+    )
+    heads_out = (numerator / denominator.T[:, :, None]).astype(jnp.bfloat16)
+    part = jnp.dot(
+        heads_out.reshape(group_len, head_width), out_weight, preferred_element_type=jnp.float32
+    ).astype(jnp.bfloat16)
+
+    owner_col = owners[:, 0]
+    target = (owner_col * (2 * slot_count) + earlier_rows(owner_col)).astype(jnp.float32)
+    target = jnp.broadcast_to(jnp.pad(target, (0, 128 - owned))[None, :], (8, 128))
+
+    delivered = pl.pallas_call(
+        merge_kernel,
+        out_shape=jax.ShapeDtypeStruct((2, tok_count, 2 * slot_count, 2 * half), jnp.bfloat16),
+        in_specs=[VMEM_SPEC] * 6,
+        out_specs=VMEM_SPEC,
+        scratch_shapes=[
+            vmem((2, 4, owned, width), jnp.bfloat16),
+            vmem((4, owned, width), jnp.bfloat16),
+            vmem((4, owned, width), jnp.bfloat16),
+            vmem((4, 4, owned, width), jnp.bfloat16),
+            vmem((4, 4, owned, 2 * half), jnp.bfloat16),
+            vmem((4, 2, owned, 2 * half), jnp.bfloat16),
+            vmem((4, owned, 2 * half), jnp.bfloat16),
+            vmem((4, owned, 2 * half), jnp.bfloat16),
+            vmem((3, 8, 128), jnp.float32),
+            vmem((2, tok_count, 2 * slot_count, 2 * half), jnp.bfloat16),
+            dma((2, 2, 4)), dma((2, 4)), dma((2, 4)), dma((2, 4)), dma((2, 4)),
+            dma((2, 4, 2)), dma((2, 4)), dma((2, 3)), dma((2, 2, tok_count)), dma((2,)),
+        ],
+        compiler_params=pltpu.CompilerParams(
+            collective_id=1, has_side_effects=True, vmem_limit_bytes=VMEM_LIMIT
+        ),
+    )(
+        part.reshape(4, 4, owned, width), residual, merge_gain.reshape(1, width),
+        merge_weight, other_weight, target,
+    )
+    delivered = delivered.reshape(2, 2, 2, 2, 2, slot_count, 2, half)
+    return delivered.transpose(0, 2, 4, 5, 1, 6, 3, 7).reshape(tok_count * slot_count, -1)
+
+
 def solution(mesh):
+    fits_blocks = mesh.shape["head"] == 4 and mesh.shape["tok"] == 8
     placed = (
         P(("tok", "head"), None),
         P(),
@@ -159,5 +573,5 @@
         P(("tok", "head"), None),
     )
     return jax.shard_map(
-        body, mesh=mesh, in_specs=placed, out_specs=P(("tok", "head"), None), check_vma=False
-    )
+        block_body if fits_blocks else body, mesh=mesh, in_specs=placed, out_specs=P(("tok", "head"), None), check_vma=False
+    )

time: 299 us -> 91.8 us (0.31)
  waiting for transfers between devices: 221 us -> 0.01 us
  Pallas kernels: 0 us -> 62.5 us
  blocking collectives: 30 us -> 0 us
  between operations: 14.7 us -> 0.18 us
  matrix products: 18.2 us -> 8.25 us
  local copies, waits for them, and re-layouts: 1.55 us -> 8.18 us
  other arithmetic: 13.2 us -> 9.19 us
    all_gather x2 -> x0, waiting for transfers between devices: 169 us -> none  [the longest x1 150 us: body(): lax.all_gather(merge_weight, 'tok', axis=1, tiled=True)]
    pallas_call x0 -> x2, Pallas kernels: none -> 62.5 us  [the longest x1 49.2 us: block_body(): pl.pallas_call(merge_kernel, out_shape=jax.ShapeDtypeStruct((2, tok_count...]
    reduce_scatter x2 -> x0, waiting for transfers between devices: 51.4 us -> none  [the longest x1 28.5 us: body(): lax.psum_scatter(jnp.dot(heads_out, out_weight, preferred_element_type=jn...]
    all_to_all x2 -> x0, blocking collectives: 30 us -> none  [the longest x1 19.8 us: body(): lax.all_to_all(send_rows, 'tok', split_axis=0, concat_axis=0, tiled=True)]
    dot_general x6 -> x4, matrix products: 18.2 us -> 8.25 us  [the longest x1 4.75 us: block_body(): lax.dot_general(normed.reshape(group_len, width), qkv_weight.reshape(3 *...]
    ppermute x0 -> x1, starting transfers between devices: none -> 3.02 us  [block_body(): lax.ppermute(merge_weight, 'tok', [(t, t ^ 2) for t in range(tok_count)])]
  transfers between devices with their start and end apart: 4 -> 1, of which waited for: 4 -> 0; matrix products, arithmetic and copies ran while one was open for 2% -> 25% of each run, Pallas kernels for 0% -> 15%
where the time goes in v1:
time: 91.8 us; the launch traced here: 91.3 us
  Pallas kernels  62.5 us (68%)
  other arithmetic  9.19 us (10%)
  matrix products  8.25 us (9%)
  local copies, waits for them, and re-layouts  8.18 us (9%)
  starting transfers between devices  3.02 us (3%)
    pallas_call x1, Pallas kernels, block_body(): pl.pallas_call(merge_kernel, out_shape=jax.ShapeDtypeStruct((2, tok_count...  49.2 us
    pallas_call x1, Pallas kernels, block_body(): pl.pallas_call(gather_kernel, out_shape=(jax.ShapeDtypeStruct((4, 4, owne...  13.4 us
    dot_general x1, matrix products, block_body(): lax.dot_general(normed.reshape(group_len, width), qkv_weight.reshape(3 *...  4.75 us
    ppermute x1, starting transfers between devices, block_body(): lax.ppermute(merge_weight, 'tok', [(t, t ^ 2) for t in range(tok_count)])  3.02 us
  transfers between devices with their start and end apart: 1, of which 0 were waited for; matrix products, arithmetic and copies ran while one was open for 25% of the time, Pallas kernels for 15%

profile of v1, /device:TPU:0, one launch (start us, length us, event | category | flops | bytes accessed | tf_op | source)
XLA Modules:
  0.0 91.3 jit_solution(4161122843280128956)
XLA Ops:
  0.0 3.0 %collective-permute-start = (bf16[1664,512]{1,0:T(8,128)(2,1)}, bf16[1664,512]{1,0:T(8,128)(2,1)S(1)}, u32[]{:S(2)}, u32[]{:S(2)}) collective-permute-start(bf16[1664,512]{1,0:T(8,128)(2,1)} %weight_ref.1), channel_id=1, source_target_pairs={{0,8},{4,12},{8,0},{12,4},{16,24},{20,28},{24,16},{28,20},{1,9},{5... | collective-permute-start | bytes 5111816 | tf_op jit(solution)/shard_map/ppermute | solution.py:466
  3.0 0.5 multiply_power_fusion
  3.6 0.8 reshape.269
  4.4 0.7 convert_element_type.42
  5.1 0.5 slice_bitcast_fusion.2
  5.7 0.7 convert_element_type.39
  6.6 1.1 %reshape.266 = bf16[32,4,1664]{2,1,0:T(4,128)(2,1)S(1)} reshape(bf16[128,1664]{1,0:T(8,128)(2,1)} %param.11) | data formatting | bytes 851968 | tf_op jit(solution)/shard_map/reshape | solution.py:480
  7.7 0.7 reshape.267.gain_ref
  8.4 13.4 %shard_map.109 = (bf16[4,4,32,1664]{3,2,1,0:T(8,128)(2,1)S(1)}, bf16[4,32,1664]{2,1,0:T(8,128)(2,1)S(1)}) custom-call(bf16[4,32,1664]{2,1,0:T(8,128)(2,1)S(1)} %bitcast.56, f32[1,1664]{1,0:T(1,128)S(1)} %reshape.267.gain_ref), custom_call_target="tpu_custom_call" | custom-call | tf_op jit(solution)/shard_map/pallas_call | solution.py:468
  21.8 4.7 %fusion.42 = f32[512,3,4,104]{0,3,2,1:T(8,128)S(1)} fusion(bf16[512,1664,1,1]{1,0,3,2:T(8,128)(2,1)S(1)} %bitcast.57, bf16[3,4,104,1664]{3,2,1,0:T(8,128)(2,1)} %bitcast.63), kind=kOutput, calls=%fused_computation.66 | convolution fusion | flops 2126512128 | bytes 8413184 | tf_op jit(solution)/shard_map/dot_general | solution.py:498
  26.6 1.5 %copy-done.3 = f32[512,3,4,104]{0,3,2,1:T(8,128)} copy-done((f32[512,3,4,104]{0,3,2,1:T(8,128)}, f32[512,3,4,104]{0,3,2,1:T(8,128)S(1)}, u32[]{:S(2)}) %copy-start.3) | copy-done | bytes 2555928
  28.1 1.3 %slice_bitcast_fusion = (f32[512,4,104]{0,2,1:T(8,128)}, f32[512,4,104]{0,2,1:T(8,128)}) fusion(f32[512,3,4,104]{0,3,2,1:T(8,128)S(1)} %fusion.42), kind=kLoop, calls=%fused_computation.15 | loop fusion | bytes 3407872 | tf_op jit(solution)/shard_map/squeeze | solution.py:507
  29.5 0.6 copy.30
  30.1 0.9 convert_reduce_fusion
  31.0 0.7 add_convert_fusion.2
  31.7 0.8 select_reduce_fusion.2
  32.5 1.2 %multiply_cosine_fusion.1 = (f32[512,26]{0,1:T(8,128)S(1)}, f32[512,26]{0,1:T(8,128)S(1)}, f32[512,26]{0,1:T(8,128)S(1)}, f32[512,26]{0,1:T(8,128)S(1)}) fusion(f32[26]{0:T(128)} %multiply_power_fusion, f32[512]{0:T(512)S(1)} %get-tuple-element.25, f32[512]{0:T(512)S(1)} %get-tuple-element.26), kind=kLoop, calls=%fused_computation.42 | loop fusion | flops 26624 | bytes 217192 | tf_op jit(solution)/shard_map/cos | solution.py:32
  33.7 1.4 %multiply_subtract_fusion.1 = (f32[512,4,26]{0,2,1:T(8,128)S(1)}, f32[512,4,26]{0,2,1:T(8,128)S(1)}, f32[512,4,26]{0,2,1:T(8,128)S(1)}, f32[512,4,26]{0,2,1:T(8,128)S(1)}) fusion(f32[512,4,104]{0,2,1:T(8,128)} %get-tuple-element.12, f32[512,26]{0,1:T(8,128)S(1)} %get-tuple-element.28, f32[512,26]{0,1:T(8,128)S(1)} %get-tuple-element.27, ...), kind=kLoop, calls=%fused_computation.38 | loop fusion | flops 638976 | bytes 1916928 | tf_op jit(solution)/shard_map/sub | solution.py:34
  35.4 0.7 fusion.20
  36.4 1.8 %fusion.41 = (f32[4,512]{1,0:T(4,128)S(1)}, bf16[4,512,512]{1,2,0:T(8,128)(2,1)S(1)}) fusion(f32[4,512,512]{1,2,0:T(8,128)S(1)} %fusion.20, pred[512,512]{0,1:T(8,128)(4,1)S(1)} %fusion.18), kind=kOutput, calls=%fused_computation.65 | output fusion | flops 6291967 | bytes 6561792 | tf_op jit(solution)/shard_map/sub | solution.py:516
  38.2 1.6 %fusion.14 = bf16[512,4,104]{0,2,1:T(8,128)(2,1)S(1)} fusion(bf16[4,512,512]{1,2,0:T(8,128)(2,1)S(1)} %get-tuple-element.36, f32[512,3,4,104]{0,3,2,1:T(8,128)} %copy-done.3, f32[512,4]{0,1:T(4,128)S(1)} %bitcast.66), kind=kOutput, calls=%fused_computation.11 | convolution fusion | flops 218529792 | bytes 2957312 | tf_op jit(solution)/shard_map/hqk,khd->qhd/dot_general | solution.py:518
  39.9 1.1 %convolution_convert_fusion = bf16[512,1664]{1,0:T(8,128)(2,1)S(1)} fusion(bf16[512,416]{0,1:T(8,128)(2,1)S(1)} %bitcast.65, bf16[416,1664]{1,0:T(8,128)(2,1)S(1)} %copy-done), kind=kOutput, calls=%fused_computation.4 | convolution fusion | flops 709689344 | bytes 3514368 | tf_op jit(solution)/shard_map/dot_general | solution.py:522
  41.3 49.2 %shard_map.110 = bf16[2,8,16,1024]{3,2,1,0:T(8,128)(2,1)S(1)} custom-call(bf16[4,4,32,1664]{3,2,1,0:T(8,128)(2,1)S(1)} %bitcast.55, bf16[4,32,1664]{2,1,0:T(8,128)(2,1)S(1)} %get-tuple-element.8.residual_ref, f32[1,1664]{1,0:T(1,128)S(1)} %reshape.272.gain_ref, bf16[1664,512]{1,0:T(8,128)(2,1)S(1)} %copy-done.1, ...), custom_call_target="tpu_custom_call" | custom-call | tf_op jit(solution)/shard_map/pallas_call | solution.py:530
  90.5 0.9 copy.33
  (27 shorter events, 1.2 us)
Async XLA Ops:
  0.0 39.9 %copy-start = (bf16[416,1664]{1,0:T(8,128)(2,1)S(1)}, bf16[416,1664]{1,0:T(8,128)(2,1)}, u32[]{:S(2)}) copy-start(bf16[416,1664]{1,0:T(8,128)(2,1)} %param.14) | copy-start | bytes 4153348
  0.0 41.0 %collective-permute-start = (bf16[1664,512]{1,0:T(8,128)(2,1)}, bf16[1664,512]{1,0:T(8,128)(2,1)S(1)}, u32[]{:S(2)}, u32[]{:S(2)}) collective-permute-start(bf16[1664,512]{1,0:T(8,128)(2,1)} %weight_ref.1), channel_id=1, source_target_pairs={{0,8},{4,12},{8,0},{12,4},{16,24},{20,28},{24,16},{28,20},{1,9},{5... | collective-permute-start | bytes 5111816 | tf_op jit(solution)/shard_map/ppermute | solution.py:466
  26.6 1.5 %copy-start.3 = (f32[512,3,4,104]{0,3,2,1:T(8,128)}, f32[512,3,4,104]{0,3,2,1:T(8,128)S(1)}, u32[]{:S(2)}) copy-start(f32[512,3,4,104]{0,3,2,1:T(8,128)S(1)} %fusion.42) | copy-start | bytes 7667716
  28.1 1.3 %copy-start.6 = (s32[512]{0:T(512)S(1)}, s32[512]{0:T(512)}, u32[]{:S(2)}) copy-start(s32[512]{0:T(512)} %param.20) | copy-start | bytes 6148
  28.1 2.1 %copy-start.4 = (f32[1664]{0:T(1024)S(1)}, f32[1664]{0:T(1024)}, u32[]{:S(2)}) copy-start(f32[1664]{0:T(1024)} %param.15) | copy-start | bytes 19972
  31.7 3.5 %copy-start.2 = (f32[512,4,104]{0,2,1:T(8,128)S(1)}, f32[512,4,104]{0,2,1:T(8,128)}, u32[]{:S(2)}) copy-start(f32[512,4,104]{0,2,1:T(8,128)} %get-tuple-element.11) | copy-start | bytes 2555908
  35.4 0.8 copy-start.5
  39.9 1.5 %copy-start.1 = (bf16[1664,512]{1,0:T(8,128)(2,1)S(1)}, bf16[1664,512]{1,0:T(8,128)(2,1)}, u32[]{:S(2)}) copy-start(bf16[1664,512]{1,0:T(8,128)(2,1)} %weight_ref.1) | copy-start | bytes 5111812

commit v2 on v1

--- a/solution.py
+++ b/solution.py
@@ -206,7 +206,7 @@
         average = jnp.mean(values, axis=-1, keepdims=True)
         centred = values - average
         variance = jnp.mean(centred * centred, axis=-1, keepdims=True)
-        normal = centred * lax.rsqrt(variance + EPSILON) * gain_ref[...]
+        normal = centred * lax.rsqrt(variance + EPSILON) * gain_ref[...][None, :]
         normed_ref[r, source] = normal.astype(jnp.bfloat16)
 
     for r in range(parts):
@@ -279,9 +279,10 @@
             sent_sum.at[c], far_sum.at[c], sum_far_sems.at[0, c], sum_far_sems.at[1, c], tok, across
         )
 
-    for c in range(chunks):
+    order = (diagonal, sibling, across, head)
+    for c in order:
         near_copy(c, 0).start()
-    for c in range(chunks):
+    for c in order:
         near_copy(c, 1).start()
     place_copies = [
         remote(
@@ -292,8 +293,7 @@
     for copy in place_copies:
         copy.start()
 
-    @pl.loop(0, chunks)
-    def _(c):
+    for c in order:
         near_copy(c, 0).wait_recv()
         total = part_ref[across, c].astype(jnp.float32) + near_sum[0, c].astype(jnp.float32)
         sent_sum[c] = total.astype(jnp.bfloat16)
@@ -317,8 +317,7 @@
 
     width = residual_ref.shape[-1]
 
-    @pl.loop(0, chunks)
-    def _(c):
+    for c in order:
         near_copy(c, 1).wait_recv()
         stream = residual_ref[c].astype(jnp.float32) + part_ref[head, c].astype(jnp.float32)
         stream = stream + near_sum[1, c].astype(jnp.float32)
@@ -326,7 +325,7 @@
         stream = stream + far_sum[c].astype(jnp.float32)
         average = jnp.sum(stream, axis=-1, keepdims=True) / width
         variance = jnp.sum(stream * stream, axis=-1, keepdims=True) / width - average * average
-        normal = (stream - average) * lax.rsqrt(variance + EPSILON) * gain_ref[...]
+        normal = (stream - average) * lax.rsqrt(variance + EPSILON) * gain_ref[...][None, :]
         rows[0, c] = normal.astype(jnp.bfloat16)
         row_z(c).start()
         row_x(c).start()
@@ -347,14 +346,16 @@
             tok, across,
         )
 
-    def project(k):
-        block = rows[k].reshape(chunks * span, width)
+    def project(k, members):
+        block = jnp.concatenate([rows[k, c] for c in members], axis=0)
         for weights, columns in ((weight_ref, own_columns), (other_ref, other_columns)):
             product = jnp.dot(block, weights[...], preferred_element_type=jnp.float32)
-            product = product.astype(jnp.bfloat16).reshape(4, owned, half)
-            terms[k, :, :, columns] = product
-        term_near(k, 0).start()
-        term_near(k, 1).start()
+            product = product.astype(jnp.bfloat16)
+            for turn, c in enumerate(members):
+                terms[k, c, :, columns] = product[turn * span : (turn + 1) * span]
+        if diagonal is members[0]:
+            term_near(k, 0).start()
+            term_near(k, 1).start()
 
     def pass_on(k):
         term_near(k, 0).wait_recv()
@@ -399,32 +400,25 @@
             delivery(which, step).start()
         kept(which).start()
 
-    project(0)
+    project(0, order)
     pass_on(0)
-
-    @pl.loop(0, chunks)
-    def _(c):
+    for c in order:
         row_x(c).wait_recv()
-
-    project(1)
+    project(1, order)
     pass_on(1)
-
-    @pl.loop(0, chunks)
-    def _(c):
+    for copy in place_copies:
+        copy.wait_recv()
+    for c in order:
         row_z(c).wait_recv()
         row_relay(c).start()
-
-    project(2)
-    pass_on(2)
-    for copy in place_copies:
-        copy.wait_recv()
     deliver(0)
-
-    @pl.loop(0, chunks)
-    def _(c):
-        row_relay(c).wait_recv()
-
-    project(3)
+    project(2, order)
+    for pair in (order[:2], order[2:]):
+        for c in pair:
+            row_relay(c).wait_recv()
+        project(3, pair)
+        if pair[0] is diagonal:
+            pass_on(2)
     pass_on(3)
     deliver(1)
 
@@ -477,7 +471,7 @@
         compiler_params=pltpu.CompilerParams(
             collective_id=0, has_side_effects=True, vmem_limit_bytes=VMEM_LIMIT
         ),
-    )(tokens.reshape(owned, 4, width).transpose(1, 0, 2), attn_gain.reshape(1, width))
+    )(tokens.reshape(owned, 4, width).transpose(1, 0, 2), attn_gain)
 
     def by_place(values):
         return values.reshape(values.shape[:-1] + (group_len // 4, 4)).swapaxes(-1, -2).reshape(
@@ -550,7 +544,7 @@
             collective_id=1, has_side_effects=True, vmem_limit_bytes=VMEM_LIMIT
         ),
     )(
-        part.reshape(4, 4, owned, width), residual, merge_gain.reshape(1, width),
+        part.reshape(4, 4, owned, width), residual, merge_gain,
         merge_weight, other_weight, target,
     )
     delivered = delivered.reshape(2, 2, 2, 2, 2, slot_count, 2, half)

time: 91.8 us -> 91.5 us (level)
  waiting for transfers between devices: 0.01 us -> 2.2 us
  other arithmetic: 9.19 us -> 7.51 us
  local copies, waits for them, and re-layouts: 8.18 us -> 6.82 us
    ppermute x1, waiting for transfers between devices: 0.01 us -> 2.2 us  [block_body(): lax.ppermute(merge_weight, 'tok', [(t, t ^ 2) for t in range(tok_count)])]
  transfers between devices with their start and end apart: 1 -> 1, of which waited for: 0 -> 1; matrix products, arithmetic and copies ran while one was open for 25% -> 21% of each run, Pallas kernels for 15% -> 15%
where the time goes in v2:
time: 91.5 us; the launch traced here: 91.1 us
  Pallas kernels  63.2 us (69%)
  matrix products  8.25 us (9%)
  other arithmetic  7.51 us (8%)
  local copies, waits for them, and re-layouts  6.82 us (7%)
  starting transfers between devices  3.02 us (3%)
  waiting for transfers between devices  2.2 us (2%)
    pallas_call x1, Pallas kernels, block_body(): pl.pallas_call(merge_kernel, out_shape=jax.ShapeDtypeStruct((2, tok_count...  49.8 us
    pallas_call x1, Pallas kernels, block_body(): pl.pallas_call(gather_kernel, out_shape=(jax.ShapeDtypeStruct((4, 4, owne...  13.4 us
    dot_general x1, matrix products, block_body(): lax.dot_general(normed.reshape(group_len, width), qkv_weight.reshape(3 *...  4.72 us
    ppermute x1, starting transfers between devices, block_body(): lax.ppermute(merge_weight, 'tok', [(t, t ^ 2) for t in range(tok_count)])  3.02 us
    unnamed x14, local copies, waits for them, and re-layouts  2.2 us
    ppermute x1, waiting for transfers between devices, block_body(): lax.ppermute(merge_weight, 'tok', [(t, t ^ 2) for t in range(tok_count)])  2.2 us
    sub x1, other arithmetic, block_body(): exponent = jnp.where(allowed[None], jnp.exp(masked - row_top), 0.0)  1.96 us
  transfers between devices with their start and end apart: 1, of which 1 were waited for; matrix products, arithmetic and copies ran while one was open for 21% of the time, Pallas kernels for 15%

profile of v2, /device:TPU:0, one launch (start us, length us, event | category | flops | bytes accessed | tf_op | source)
XLA Modules:
  0.0 91.1 jit_solution(10405299957528695390)
XLA Ops:
  0.0 3.0 %collective-permute-start = (bf16[1664,512]{1,0:T(8,128)(2,1)}, bf16[1664,512]{1,0:T(8,128)(2,1)S(1)}, u32[]{:S(2)}, u32[]{:S(2)}) collective-permute-start(bf16[1664,512]{1,0:T(8,128)(2,1)} %weight_ref.1), channel_id=1, source_target_pairs={{0,8},{4,12},{8,0},{12,4},{16,24},{20,28},{24,16},{28,20},{1,9},{5... | collective-permute-start | bytes 5111816 | tf_op jit(solution)/shard_map/ppermute | solution.py:460
  3.0 0.8 reshape.262
  3.9 0.7 convert_element_type.42
  4.6 0.7 convert_element_type.39
  5.3 0.1 convert_element_type.40
  5.5 1.1 %reshape.260 = bf16[32,4,1664]{2,1,0:T(4,128)(2,1)S(1)} reshape(bf16[128,1664]{1,0:T(8,128)(2,1)} %param.11) | data formatting | bytes 851968 | tf_op jit(solution)/shard_map/reshape | solution.py:474
  6.7 0.7 copy-done.3
  7.4 13.4 %shard_map.109 = (bf16[4,4,32,1664]{3,2,1,0:T(8,128)(2,1)S(1)}, bf16[4,32,1664]{2,1,0:T(8,128)(2,1)S(1)}) custom-call(bf16[4,32,1664]{2,1,0:T(8,128)(2,1)S(1)} %bitcast.55, f32[1664]{0:T(1024)S(1)} %copy-done.3), custom_call_target="tpu_custom_call" | custom-call | tf_op jit(solution)/shard_map/pallas_call | solution.py:462
  20.8 4.7 %fusion.42 = f32[512,3,4,104]{0,3,2,1:T(8,128)S(1)} fusion(bf16[512,1664,1,1]{1,0,3,2:T(8,128)(2,1)S(1)} %bitcast.57, bf16[3,4,104,1664]{3,2,1,0:T(8,128)(2,1)} %bitcast.63), kind=kOutput, calls=%fused_computation.66 | convolution fusion | flops 2126512128 | bytes 8413184 | tf_op jit(solution)/shard_map/dot_general | solution.py:492
  25.5 1.5 %copy-done.5 = f32[512,3,4,104]{0,3,2,1:T(8,128)} copy-done((f32[512,3,4,104]{0,3,2,1:T(8,128)}, f32[512,3,4,104]{0,3,2,1:T(8,128)S(1)}, u32[]{:S(2)}) %copy-start.5) | copy-done | bytes 2555928
  27.0 1.3 %slice_bitcast_fusion = (f32[512,4,104]{0,2,1:T(8,128)}, f32[512,4,104]{0,2,1:T(8,128)}) fusion(f32[512,3,4,104]{0,3,2,1:T(8,128)S(1)} %fusion.42), kind=kLoop, calls=%fused_computation.15 | loop fusion | bytes 3407872 | tf_op jit(solution)/shard_map/squeeze | solution.py:501
  28.5 0.9 %convert_reduce_fusion = s32[32]{0:T(128)S(1)} fusion(s32[32]{0:T(128)} %bitcast.64), kind=kLoop, calls=%fused_computation.43 | loop fusion | flops 5088 | bytes 256 | tf_op jit(solution)/shard_map/reduce_sum | solution.py:42
  29.4 0.7 add_convert_fusion.2
  30.2 0.5 multiply_cosine_fusion.1
  30.8 1.4 %multiply_subtract_fusion.1 = (f32[512,4,26]{0,2,1:T(8,128)S(1)}, f32[512,4,26]{0,2,1:T(8,128)S(1)}, f32[512,4,26]{0,2,1:T(8,128)S(1)}, f32[512,4,26]{0,2,1:T(8,128)S(1)}) fusion(f32[512,4,104]{0,2,1:T(8,128)} %get-tuple-element.12, f32[512,26]{0,1:T(8,128)S(1)} %get-tuple-element.28, f32[512,26]{0,1:T(8,128)S(1)} %get-tuple-element.27, ...), kind=kLoop, calls=%fused_computation.38 | loop fusion | flops 638976 | bytes 1916928 | tf_op jit(solution)/shard_map/sub | solution.py:34
  32.2 0.2 subtract_convert_fusion.1
  32.4 0.7 fusion.20
  33.2 0.3 fusion.18
  33.4 2.0 %fusion.41 = (f32[4,512]{1,0:T(4,128)S(1)}, bf16[4,512,512]{1,2,0:T(8,128)(2,1)S(1)}) fusion(f32[4,512,512]{1,2,0:T(8,128)S(1)} %fusion.20, pred[512,512]{0,1:T(8,128)(4,1)S(1)} %fusion.18), kind=kOutput, calls=%fused_computation.65 | output fusion | flops 6291967 | bytes 6561792 | tf_op jit(solution)/shard_map/sub | solution.py:510
  35.4 1.6 %fusion.14 = bf16[512,4,104]{0,2,1:T(8,128)(2,1)S(1)} fusion(bf16[4,512,512]{1,2,0:T(8,128)(2,1)S(1)} %get-tuple-element.36, f32[512,3,4,104]{0,3,2,1:T(8,128)} %copy-done.5, f32[512,4]{0,1:T(4,128)S(1)} %bitcast.66), kind=kOutput, calls=%fused_computation.11 | convolution fusion | flops 218529792 | bytes 2957312 | tf_op jit(solution)/shard_map/hqk,khd->qhd/dot_general | solution.py:512
  37.1 1.2 %convolution_convert_fusion = bf16[512,1664]{1,0:T(8,128)(2,1)S(1)} fusion(bf16[512,416]{0,1:T(8,128)(2,1)S(1)} %bitcast.65, bf16[416,1664]{1,0:T(8,128)(2,1)S(1)} %copy-done), kind=kOutput, calls=%fused_computation.4 | convolution fusion | flops 709689344 | bytes 3514368 | tf_op jit(solution)/shard_map/dot_general | solution.py:516
  38.2 2.2 %collective-permute-done.other_ref = bf16[1664,512]{1,0:T(8,128)(2,1)S(1)} collective-permute-done((bf16[1664,512]{1,0:T(8,128)(2,1)}, bf16[1664,512]{1,0:T(8,128)(2,1)S(1)}, u32[]{:S(2)}, u32[]{:S(2)}) %collective-permute-start) | collective-permute-done | bytes 1703968 | tf_op jit(solution)/shard_map/ppermute | solution.py:460
  40.4 49.8 %shard_map.110 = bf16[2,8,16,1024]{3,2,1,0:T(8,128)(2,1)S(1)} custom-call(bf16[4,4,32,1664]{3,2,1,0:T(8,128)(2,1)S(1)} %bitcast.56, bf16[4,32,1664]{2,1,0:T(8,128)(2,1)S(1)} %get-tuple-element.8.residual_ref, f32[1664]{0:T(1024)S(1)} %copy-done.2, bf16[1664,512]{1,0:T(8,128)(2,1)S(1)} %copy-done.1, bf16[1664,512]{1,0:T(8,128)(2,1)S(1)} %collective-permute-done.other_ref, ...), custom_call_target="tpu_custom_call" | custom-call | tf_op jit(solution)/shard_map/pallas_call | solution.py:524
  90.3 0.9 copy.33
  (25 shorter events, 0.5 us)
Async XLA Ops:
  0.0 37.0 %copy-start = (bf16[416,1664]{1,0:T(8,128)(2,1)S(1)}, bf16[416,1664]{1,0:T(8,128)(2,1)}, u32[]{:S(2)}) copy-start(bf16[416,1664]{1,0:T(8,128)(2,1)} %param.14) | copy-start | bytes 4153348
  0.0 40.4 %collective-permute-start = (bf16[1664,512]{1,0:T(8,128)(2,1)}, bf16[1664,512]{1,0:T(8,128)(2,1)S(1)}, u32[]{:S(2)}, u32[]{:S(2)}) collective-permute-start(bf16[1664,512]{1,0:T(8,128)(2,1)} %weight_ref.1), channel_id=1, source_target_pairs={{0,8},{4,12},{8,0},{12,4},{16,24},{20,28},{24,16},{28,20},{1,9},{5... | collective-permute-start | bytes 5111816 | tf_op jit(solution)/shard_map/ppermute | solution.py:460
  6.7 0.7 copy-start.3
  25.5 1.5 %copy-start.5 = (f32[512,3,4,104]{0,3,2,1:T(8,128)}, f32[512,3,4,104]{0,3,2,1:T(8,128)S(1)}, u32[]{:S(2)}) copy-start(f32[512,3,4,104]{0,3,2,1:T(8,128)S(1)} %fusion.42) | copy-start | bytes 7667716
  27.0 1.3 %copy-start.6 = (s32[512]{0:T(512)S(1)}, s32[512]{0:T(512)}, u32[]{:S(2)}) copy-start(s32[512]{0:T(512)} %param.20) | copy-start | bytes 6148
  30.1 2.1 %copy-start.4 = (f32[512,4,104]{0,2,1:T(8,128)S(1)}, f32[512,4,104]{0,2,1:T(8,128)}, u32[]{:S(2)}) copy-start(f32[512,4,104]{0,2,1:T(8,128)} %get-tuple-element.11) | copy-start | bytes 2555908
  37.1 3.4 %copy-start.1 = (bf16[1664,512]{1,0:T(8,128)(2,1)S(1)}, bf16[1664,512]{1,0:T(8,128)(2,1)}, u32[]{:S(2)}) copy-start(bf16[1664,512]{1,0:T(8,128)(2,1)} %weight_ref.1) | copy-start | bytes 5111812
  37.1 3.4 %copy-start.2 = (f32[1664]{0:T(1024)S(1)}, f32[1664]{0:T(1024)}, u32[]{:S(2)}) copy-start(f32[1664]{0:T(1024)} %gain_ref.3) | copy-start | bytes 19972

commit v3 on v2

--- a/solution.py
+++ b/solution.py
@@ -178,77 +178,12 @@
     return tok, head, sibling, across
 
 
-def gather_kernel(
-    tokens_ref, gain_ref, normed_ref, residual_ref, raw, own_sems, across_sems, relay_sems
-):
-    tok, head, sibling, across = head_partners()
-    diagonal = (sibling + 2) % 4
-    parts = tokens_ref.shape[0]
-    greet([(tok, sibling), (tok, across)])
-
-    def to_across(r):
-        return remote(
-            tokens_ref.at[r], raw.at[1, r], across_sems.at[0, r], across_sems.at[1, r], tok, across
-        )
-
-    def to_sibling(r):
-        return remote(
-            tokens_ref.at[r], raw.at[0, r], own_sems.at[0, r], own_sems.at[1, r], tok, sibling
-        )
-
-    def relay(r):
-        return remote(
-            raw.at[1, r], raw.at[2, r], relay_sems.at[0, r], relay_sems.at[1, r], tok, sibling
-        )
-
-    def settle(rows, r, source):
-        values = rows.astype(jnp.float32)
-        average = jnp.mean(values, axis=-1, keepdims=True)
-        centred = values - average
-        variance = jnp.mean(centred * centred, axis=-1, keepdims=True)
-        normal = centred * lax.rsqrt(variance + EPSILON) * gain_ref[...][None, :]
-        normed_ref[r, source] = normal.astype(jnp.bfloat16)
-
-    for r in range(parts):
-        to_across(r).start()
-    for r in range(parts):
-        to_sibling(r).start()
-
-    @pl.loop(0, parts)
-    def _(r):
-        settle(tokens_ref[r], r, head)
-
-    @pl.loop(0, parts)
-    def _(r):
-        to_sibling(r).wait_recv()
-        settle(raw[0, r], r, sibling)
-
-    @pl.loop(0, parts)
-    def _(r):
-        to_across(r).wait_recv()
-        relay(r).start()
-        settle(raw[1, r], r, across)
-
-    @pl.loop(0, parts)
-    def _(r):
-        relay(r).wait_recv()
-        settle(raw[2, r], r, diagonal)
-
-    residual_ref[head] = tokens_ref[head]
-    residual_ref[sibling] = raw[0, head]
-    residual_ref[across] = raw[1, head]
-    residual_ref[diagonal] = raw[2, head]
-
-    @pl.loop(0, parts)
-    def _(r):
-        to_across(r).wait_send()
-        to_sibling(r).wait_send()
-        relay(r).wait_send()
-
-
-def merge_kernel(
-    part_ref, residual_ref, gain_ref, weight_ref, other_ref, target_ref, out_ref,
+def layer_kernel(
+    tokens_ref, attn_gain_ref, gain_ref, turns_ref, lanes_ref, columns_ref, target_ref,
+    qkv_hbm, out_hbm, merge_hbm, out_ref,
+    qkv_ref, outw_ref, weight_ref, other_ref, raw, normed, residual_ref, queries, keys, held, tables, part_ref,
     near_sum, sent_sum, far_sum, rows, terms, near_term, sent_term, far_term, places, messages,
+    load_sems, weight_sems, own_sems, across_sems, relay_sems,
     sum_near_sems, sum_far_sems, row_x_sems, row_z_sems, row_relay_sems,
     term_near_sems, term_far_sems, place_sems, out_sems, local_sems,
 ):
@@ -257,33 +192,48 @@
     toks = lax.axis_size("tok")
     p, q, x = tok // 4, (tok // 2) % 2, tok % 2
     beside = tok + 1 - 2 * x
+    paired = tok + 2 - 4 * q
     over = (tok + 4) % 8
     corner = (beside + 4) % 8
     span = near_sum.shape[2]
     chunks = part_ref.shape[1]
     owned = near_term.shape[2]
     half = weight_ref.shape[1]
+    width = residual_ref.shape[-1]
+    local = chunks * span
+    loads = [
+        pltpu.make_async_copy(source, target, load_sems.at[i])
+        for i, (source, target) in enumerate(
+            ((qkv_hbm, qkv_ref), (out_hbm, outw_ref), (merge_hbm, weight_ref))
+        )
+    ]
+    for load in loads:
+        load.start()
     greet(
         [((tok + step) % toks, head) for step in range(1, toks)] + [(tok, sibling), (tok, across)]
     )
 
-    def near_copy(c, which):
-        block = (diagonal, sibling)[which]
-        return remote(
-            part_ref.at[block, c], near_sum.at[which, c],
-            sum_near_sems.at[0, which, c], sum_near_sems.at[1, which, c], tok, sibling,
-        )
-
-    def far_copy(c):
-        return remote(
-            sent_sum.at[c], far_sum.at[c], sum_far_sems.at[0, c], sum_far_sems.at[1, c], tok, across
-        )
-
-    order = (diagonal, sibling, across, head)
-    for c in order:
-        near_copy(c, 0).start()
-    for c in order:
-        near_copy(c, 1).start()
+    def to_across(r):
+        return remote(
+            tokens_ref.at[r], raw.at[1, r], across_sems.at[0, r], across_sems.at[1, r], tok, across
+        )
+
+    def to_sibling(r):
+        return remote(
+            tokens_ref.at[r], raw.at[0, r], own_sems.at[0, r], own_sems.at[1, r], tok, sibling
+        )
+
+    def relay(r):
+        return remote(
+            raw.at[1, r], raw.at[2, r], relay_sems.at[0, r], relay_sems.at[1, r], tok, sibling
+        )
+
+    for r in range(chunks):
+        to_across(r).start()
+    for r in range(chunks):
+        to_sibling(r).start()
+    weight_copy = remote(merge_hbm, other_ref, weight_sems.at[0], weight_sems.at[1], paired, head)
+    weight_copy.start()
     place_copies = [
         remote(
             target_ref, places.at[k], place_sems.at[0, k], place_sems.at[1, k], device, head
@@ -293,31 +243,139 @@
     for copy in place_copies:
         copy.start()
 
-    for c in order:
+    heads_here = queries.shape[0]
+    angles = jnp.where(turns_ref[:, 1:2] == 0.0, lanes_ref[0:1, :], lanes_ref[1:2, :])
+    angles = angles * turns_ref[:, 0:1]
+    cosine = jnp.cos(angles)
+    sine = jnp.sin(angles) * turns_ref[:, 2:3]
+    tables[0] = cosine
+    tables[1] = sine
+    row_places = lax.broadcasted_iota(jnp.int32, (span, local), 0)
+    token_places = lax.broadcasted_iota(jnp.int32, (span, local), 1)
+    own_rows = jnp.where(token_places == 4 * row_places + head, 1.0, 0.0).astype(jnp.bfloat16)
+    spread = lax.broadcasted_iota(jnp.int32, (local, local), 0)
+    spread = 4 * (spread % span) + spread // span
+    by_place = jnp.where(
+        lax.broadcasted_iota(jnp.int32, (local, local), 1) == spread, 1.0, 0.0
+    ).astype(jnp.bfloat16)
+
+    def settle(piece, r):
+        values = piece.astype(jnp.float32)
+        average = jnp.mean(values, axis=-1, keepdims=True)
+        centred = values - average
+        variance = jnp.mean(centred * centred, axis=-1, keepdims=True)
+        normal = centred * lax.rsqrt(variance + EPSILON) * attn_gain_ref[...][None, :]
+        normed[r] = normal.astype(jnp.bfloat16)
+
+    def spin(values, lanes, factor):
+        quarter = HD // 4
+        a, b, c, d = (values[i * quarter : (i + 1) * quarter] for i in range(4))
+        swapped = jnp.concatenate([b, a, d, c], axis=0)
+        return (values * tables[0, :, lanes] + swapped * tables[1, :, lanes]) * factor
+
+    def take_in(source, whole):
+        residual_ref[source] = jnp.dot(
+            own_rows, whole, preferred_element_type=jnp.float32
+        ).astype(jnp.bfloat16)
+        lanes = pl.ds(pl.multiple_of(source * local, local), local)
+        block = normed[...].reshape(local, width)
+        for which in range(3):
+            product = lax.dot_general(
+                qkv_ref[which], block, (((1,), (1,)), ((), ())), preferred_element_type=jnp.float32
+            )
+            for n in range(heads_here):
+                values = product[n * HD : (n + 1) * HD]
+                if which == 0:
+                    queries[n, :, lanes] = spin(values, lanes, HD ** (-0.5)).astype(jnp.bfloat16)
+                elif which == 1:
+                    keys[n, lanes, :] = spin(values, lanes, 1.0).T.astype(jnp.bfloat16)
+                else:
+                    held[n, :, lanes] = values.astype(jnp.bfloat16)
+
+    for r in range(chunks):
+        settle(tokens_ref[r], r)
+    loads[0].wait()
+    take_in(head, tokens_ref[...].reshape(local, width))
+    for r in range(chunks):
+        to_sibling(r).wait_recv()
+        settle(raw[0, r], r)
+    take_in(sibling, raw[0].reshape(local, width))
+    for r in range(chunks):
+        to_across(r).wait_recv()
+        relay(r).start()
+        settle(raw[1, r], r)
+    take_in(across, raw[1].reshape(local, width))
+    for r in range(chunks):
+        relay(r).wait_recv()
+        settle(raw[2, r], r)
+    take_in(diagonal, raw[2].reshape(local, width))
+    loads[1].wait()
+
+    def attend(c):
+        lanes = pl.ds(pl.multiple_of(c * local, local), local)
+        group = columns_ref.shape[0]
+        key_places = lax.broadcasted_iota(jnp.int32, (group, local), 0)
+        query_places = lax.broadcasted_iota(jnp.int32, (group, local), 1) + c * local
+        allowed = (columns_ref[:, 0:1] == lanes_ref[2:3, lanes]) & (
+            (columns_ref[:, 1:2] == 1.0) | (key_places == query_places)
+        )
+        pieces = []
+        for n in range(heads_here):
+            scores = jnp.dot(keys[n], queries[n, :, lanes], preferred_element_type=jnp.float32)
+            masked = jnp.where(allowed, scores, NEGATIVE)
+            top = jnp.max(masked, axis=0, keepdims=True)
+            exponent = jnp.where(allowed, jnp.exp(masked - top), 0.0)
+            total = jnp.sum(exponent, axis=0, keepdims=True)
+            numerator = jnp.dot(
+                held[n], exponent.astype(jnp.bfloat16), preferred_element_type=jnp.float32
+            )
+            pieces.append(numerator / total)
+        heads_out = jnp.concatenate(pieces, axis=0).astype(jnp.bfloat16)
+        ordered = lax.dot_general(
+            by_place, heads_out, (((1,), (1,)), ((), ())), preferred_element_type=jnp.float32
+        ).astype(jnp.bfloat16)
+        part = jnp.dot(ordered, outw_ref[...], preferred_element_type=jnp.float32)
+        part = part.astype(jnp.bfloat16)
+        for r in range(4):
+            part_ref[r, c] = part[r * span : (r + 1) * span]
+
+    def near_copy(c, which):
+        block = (diagonal, sibling)[which]
+        return remote(
+            part_ref.at[block, c], near_sum.at[which, c],
+            sum_near_sems.at[0, which, c], sum_near_sems.at[1, which, c], tok, sibling,
+        )
+
+    def far_copy(c):
+        return remote(
+            sent_sum.at[c], far_sum.at[c], sum_far_sems.at[0, c], sum_far_sems.at[1, c], tok, across
+        )
+
+    order = (0, 1, 2, 3)
+
+    def row_x(c):
+        return remote(
+            rows.at[0, c], rows.at[1, c], row_x_sems.at[0, c], row_x_sems.at[1, c], beside, head
+        )
+
+    def row_z(c):
+        return remote(
+            rows.at[0, c], rows.at[2, c], row_z_sems.at[0, c], row_z_sems.at[1, c], over, head
+        )
+
+    def row_relay(c):
+        return remote(
+            rows.at[2, c], rows.at[3, c],
+            row_relay_sems.at[0, c], row_relay_sems.at[1, c], beside, head,
+        )
+
+    def pair_sum(c):
         near_copy(c, 0).wait_recv()
         total = part_ref[across, c].astype(jnp.float32) + near_sum[0, c].astype(jnp.float32)
         sent_sum[c] = total.astype(jnp.bfloat16)
         far_copy(c).start()
 
-    def row_x(c):
-        return remote(
-            rows.at[0, c], rows.at[1, c], row_x_sems.at[0, c], row_x_sems.at[1, c], beside, head
-        )
-
-    def row_z(c):
-        return remote(
-            rows.at[0, c], rows.at[2, c], row_z_sems.at[0, c], row_z_sems.at[1, c], over, head
-        )
-
-    def row_relay(c):
-        return remote(
-            rows.at[2, c], rows.at[3, c],
-            row_relay_sems.at[0, c], row_relay_sems.at[1, c], beside, head,
-        )
-
-    width = residual_ref.shape[-1]
-
-    for c in order:
+    def merge_rows(c):
         near_copy(c, 1).wait_recv()
         stream = residual_ref[c].astype(jnp.float32) + part_ref[head, c].astype(jnp.float32)
         stream = stream + near_sum[1, c].astype(jnp.float32)
@@ -330,6 +388,18 @@
         row_z(c).start()
         row_x(c).start()
 
+    for turn, c in enumerate(order):
+        attend(c)
+        near_copy(c, 0).start()
+        near_copy(c, 1).start()
+        if turn >= 1:
+            pair_sum(order[turn - 1])
+        if turn >= 2:
+            merge_rows(order[turn - 2])
+    pair_sum(order[-1])
+    merge_rows(order[-2])
+    merge_rows(order[-1])
+
     own_columns = pl.ds(pl.multiple_of(q * half, half), half)
     other_columns = pl.ds(pl.multiple_of((1 - q) * half, half), half)
 
@@ -353,7 +423,7 @@
             product = product.astype(jnp.bfloat16)
             for turn, c in enumerate(members):
                 terms[k, c, :, columns] = product[turn * span : (turn + 1) * span]
-        if diagonal is members[0]:
+        if members[-1] == order[-1]:
             term_near(k, 0).start()
             term_near(k, 1).start()
 
@@ -400,6 +470,8 @@
             delivery(which, step).start()
         kept(which).start()
 
+    loads[2].wait()
+    weight_copy.wait_recv()
     project(0, order)
     pass_on(0)
     for c in order:
@@ -417,13 +489,16 @@
         for c in pair:
             row_relay(c).wait_recv()
         project(3, pair)
-        if pair[0] is diagonal:
+        if pair[0] == order[0]:
             pass_on(2)
     pass_on(3)
     deliver(1)
 
     @pl.loop(0, chunks)
     def _(c):
+        to_across(c).wait_send()
+        to_sibling(c).wait_send()
+        relay(c).wait_send()
         near_copy(c, 0).wait_send()
         near_copy(c, 1).wait_send()
         far_copy(c).wait_send()
@@ -431,6 +506,7 @@
         row_z(c).wait_send()
         row_relay(c).wait_send()
 
+    weight_copy.wait_send()
     for copy in place_copies:
         copy.wait_send()
     for k in range(4):
@@ -457,30 +533,8 @@
     slot_count = 2 * owned // tok_count
     dma, vmem = pltpu.SemaphoreType.DMA, pltpu.VMEM
 
-    other_weight = lax.ppermute(merge_weight, "tok", [(t, t ^ 2) for t in range(tok_count)])
-
-    normed, residual = pl.pallas_call(
-        gather_kernel,
-        out_shape=(
-            jax.ShapeDtypeStruct((4, 4, owned, width), jnp.bfloat16),
-            jax.ShapeDtypeStruct((4, owned, width), jnp.bfloat16),
-        ),
-        in_specs=[VMEM_SPEC] * 2,
-        out_specs=(VMEM_SPEC, VMEM_SPEC),
-        scratch_shapes=[vmem((3, 4, owned, width), jnp.bfloat16)] + [dma((2, 4))] * 3,
-        compiler_params=pltpu.CompilerParams(
-            collective_id=0, has_side_effects=True, vmem_limit_bytes=VMEM_LIMIT
-        ),
-    )(tokens.reshape(owned, 4, width).transpose(1, 0, 2), attn_gain)
-
-    def by_place(values):
-        return values.reshape(values.shape[:-1] + (group_len // 4, 4)).swapaxes(-1, -2).reshape(
-            values.shape
-        )
-
-    segments = by_place(segment_ids)
-    key_live = by_place(live_mask) == 1
-    places = by_place(patch_pos).astype(jnp.float32)
+    segments, key_live = segment_ids, live_mask
+    places = patch_pos.astype(jnp.float32)
     image_count = grid_sizes.shape[1]
     local_image = segments - lax.axis_index("tok") * image_count
     image_match = local_image[:, None] == jnp.arange(image_count, dtype=jnp.int32)[None, :]
@@ -489,44 +543,44 @@
     col_size = jnp.sum(jnp.where(image_match, grid_float[1][None, :], 0.0), axis=1)
     row_coord = places[0] * SIDE / row_size
     col_coord = places[1] * SIDE / col_size
-    projected_rows = lax.dot_general(
-        normed.reshape(group_len, width),
-        qkv_weight.reshape(3 * head_width, width),
-        (((1,), (1,)), ((), ())),
-        preferred_element_type=jnp.float32,
-    ).reshape(group_len, 3, heads_here, HD)
-    queries = (rotate(projected_rows[:, 0], row_coord, col_coord) * HD ** (-0.5)).astype(
-        jnp.bfloat16
-    )
-    keys = rotate(projected_rows[:, 1], row_coord, col_coord).astype(jnp.bfloat16)
-    values = projected_rows[:, 2].astype(jnp.bfloat16)
-    order = jnp.arange(group_len, dtype=jnp.int32)
-    allowed = (segments[:, None] == segments[None, :]) & (
-        key_live[None, :] | (order[:, None] == order[None, :])
-    )
-    scores = jnp.einsum("qhd,khd->hqk", queries, keys, preferred_element_type=jnp.float32)
-    masked = jnp.where(allowed[None], scores, NEGATIVE)
-    row_top = jnp.max(masked, axis=2, keepdims=True)
-    exponent = jnp.where(allowed[None], jnp.exp(masked - row_top), 0.0)
-    denominator = jnp.sum(exponent, axis=2)
-    numerator = jnp.einsum(
-        "hqk,khd->qhd", exponent.astype(jnp.bfloat16), values, preferred_element_type=jnp.float32
-    )
-    heads_out = (numerator / denominator.T[:, :, None]).astype(jnp.bfloat16)
-    part = jnp.dot(
-        heads_out.reshape(group_len, head_width), out_weight, preferred_element_type=jnp.float32
-    ).astype(jnp.bfloat16)
+    segment_float = local_image.astype(jnp.float32)
+    lanes = jnp.stack([row_coord, col_coord, segment_float, jnp.zeros_like(row_coord)])
+    columns = jnp.stack([segment_float, key_live.astype(jnp.float32)], axis=1)
+    quarter = HD // 4
+    frequency = 10000.0 ** (-jnp.arange(quarter, dtype=jnp.float32) / quarter)
+    fourth = jnp.arange(HD, dtype=jnp.int32) // quarter
+    turns = jnp.stack(
+        [
+            jnp.tile(frequency, 4),
+            (fourth // 2).astype(jnp.float32),
+            (2 * (fourth % 2) - 1).astype(jnp.float32),
+        ],
+        axis=1,
+    )
 
     owner_col = owners[:, 0]
     target = (owner_col * (2 * slot_count) + earlier_rows(owner_col)).astype(jnp.float32)
     target = jnp.broadcast_to(jnp.pad(target, (0, 128 - owned))[None, :], (8, 128))
 
+    hbm = pl.BlockSpec(memory_space=pl.ANY)
     delivered = pl.pallas_call(
-        merge_kernel,
+        layer_kernel,
         out_shape=jax.ShapeDtypeStruct((2, tok_count, 2 * slot_count, 2 * half), jnp.bfloat16),
-        in_specs=[VMEM_SPEC] * 6,
+        in_specs=[VMEM_SPEC] * 7 + [hbm] * 3,
         out_specs=VMEM_SPEC,
         scratch_shapes=[
+            vmem((3, head_width, width), jnp.bfloat16),
+            vmem((head_width, width), jnp.bfloat16),
+            vmem((width, half), jnp.bfloat16),
+            vmem((width, half), jnp.bfloat16),
+            vmem((3, 4, owned, width), jnp.bfloat16),
+            vmem((4, owned, width), jnp.bfloat16),
+            vmem((4, owned, width), jnp.bfloat16),
+            vmem((heads_here, HD, group_len), jnp.bfloat16),
+            vmem((heads_here, group_len, HD), jnp.bfloat16),
+            vmem((heads_here, HD, group_len), jnp.bfloat16),
+            vmem((2, HD, group_len), jnp.float32),
+            vmem((4, 4, owned, width), jnp.bfloat16),
             vmem((2, 4, owned, width), jnp.bfloat16),
             vmem((4, owned, width), jnp.bfloat16),
             vmem((4, owned, width), jnp.bfloat16),
@@ -537,15 +591,16 @@
             vmem((4, owned, 2 * half), jnp.bfloat16),
             vmem((3, 8, 128), jnp.float32),
             vmem((2, tok_count, 2 * slot_count, 2 * half), jnp.bfloat16),
+            dma((3,)), dma((2,)), dma((2, 4)), dma((2, 4)), dma((2, 4)),
             dma((2, 2, 4)), dma((2, 4)), dma((2, 4)), dma((2, 4)), dma((2, 4)),
             dma((2, 4, 2)), dma((2, 4)), dma((2, 3)), dma((2, 2, tok_count)), dma((2,)),
         ],
         compiler_params=pltpu.CompilerParams(
-            collective_id=1, has_side_effects=True, vmem_limit_bytes=VMEM_LIMIT
+            collective_id=0, has_side_effects=True, vmem_limit_bytes=VMEM_LIMIT
         ),
     )(
-        part.reshape(4, 4, owned, width), residual, merge_gain,
-        merge_weight, other_weight, target,
+        tokens.reshape(4, owned, width), attn_gain, merge_gain, turns, lanes, columns, target,
+        qkv_weight, out_weight, merge_weight,
     )
     delivered = delivered.reshape(2, 2, 2, 2, 2, slot_count, 2, half)
     return delivered.transpose(0, 2, 4, 5, 1, 6, 3, 7).reshape(tok_count * slot_count, -1)

time: 91.5 us -> 94.7 us (1.035)
  Pallas kernels: 63.2 us -> 83.3 us
  matrix products: 8.25 us -> 0 us
  starting transfers between devices: 3.02 us -> 0 us
  other arithmetic: 7.51 us -> 4.55 us
  waiting for transfers between devices: 2.2 us -> 0 us
    pallas_call x2 -> x1, Pallas kernels: 63.2 us -> 83.3 us  [block_body(): pl.pallas_call(layer_kernel, out_shape=jax.ShapeDtypeStruct((2, tok_count...]
    dot_general x4 -> x0, matrix products: 8.25 us -> none  [the longest x1 4.72 us: block_body(): lax.dot_general(normed.reshape(group_len, width), qkv_weight.reshape(3 *...]
    sub x3 -> x0, other arithmetic: 3.4 us -> none  [the longest x1 1.96 us: block_body(): exponent = jnp.where(allowed[None], jnp.exp(masked - row_top), 0.0)]
    ppermute x1 -> x0, starting transfers between devices: 3.02 us -> none  [block_body(): lax.ppermute(merge_weight, 'tok', [(t, t ^ 2) for t in range(tok_count)])]
    unnamed x14 -> x10, local copies, waits for them, and re-layouts: 2.2 us -> 5.19 us
    ppermute x1 -> x0, waiting for transfers between devices: 2.2 us -> none  [block_body(): lax.ppermute(merge_weight, 'tok', [(t, t ^ 2) for t in range(tok_count)])]
    reshape x3 -> x0, local copies, waits for them, and re-layouts: 1.96 us -> none  [the longest x2 1.17 us: block_body(): tokens.reshape(owned, 4, width).transpose(1, 0, 2)]
    convert_element_type x1 -> x4, other arithmetic: 0.69 us -> 2.08 us  [the longest x1 0.69 us: block_body(): places = patch_pos.astype(jnp.float32)]
  transfers between devices with their start and end apart: 1 -> 0, of which waited for: 1 -> 0; matrix products, arithmetic and copies ran while one was open for 21% -> 0% of each run, Pallas kernels for 15% -> 0%
where the time goes in v3:
time: 94.7 us; the launch traced here: 94.3 us
  Pallas kernels  83.3 us (88%)
  local copies, waits for them, and re-layouts  6.48 us (7%)
  other arithmetic  4.55 us (5%)
    pallas_call x1, Pallas kernels, block_body(): pl.pallas_call(layer_kernel, out_shape=jax.ShapeDtypeStruct((2, tok_count...  83.3 us
    unnamed x10, local copies, waits for them, and re-layouts  5.19 us

profile of v3, /device:TPU:0, one launch (start us, length us, event | category | flops | bytes accessed | tf_op | source)
XLA Modules:
  0.0 94.3 jit_solution(17591691104032847421)
XLA Ops:
  0.0 0.9 convert_reduce_fusion
  0.9 0.7 add_convert_fusion
  1.6 0.1 pad.10.clone
  1.7 0.7 convert_element_type.43
  2.4 0.1 stack_tile.3
  2.5 0.7 convert_element_type.45
  3.2 0.7 fusion.7
  3.9 0.1 select_reduce_fusion.1
  4.0 0.7 convert_element_type.42
  4.7 0.1 maximum_maximum_fusion.lanes_ref
  4.7 0.1 copy.21.turns_ref
  4.9 0.1 copy.22.columns_ref
  5.0 0.0 copy-start
  5.0 1.4 %copy-done = bf16[1664,512]{1,0:T(8,128)(2,1)S(1)} copy-done((bf16[1664,512]{1,0:T(8,128)(2,1)S(1)}, bf16[1664,512]{1,0:T(8,128)(2,1)}, u32[]{:S(2)}) %copy-start) | copy-done | bytes 1703960
  6.5 0.0 copy-start.1
  6.5 1.3 %copy-done.1 = bf16[416,1664]{1,0:T(8,128)(2,1)S(1)} copy-done((bf16[416,1664]{1,0:T(8,128)(2,1)S(1)}, bf16[416,1664]{1,0:T(8,128)(2,1)}, u32[]{:S(2)}) %copy-start.1) | copy-done | bytes 1384472
  7.8 0.0 copy-start.2
  7.8 1.0 %copy-done.2 = bf16[128,1664]{1,0:T(8,128)(2,1)S(1)} copy-done((bf16[128,1664]{1,0:T(8,128)(2,1)S(1)}, bf16[128,1664]{1,0:T(8,128)(2,1)}, u32[]{:S(2)}) %copy-start.2) | copy-done | bytes 426008
  8.8 0.0 copy-start.3
  8.8 0.7 copy-done.3
  9.5 0.0 copy-start.4
  9.5 0.7 copy-done.4
  10.2 83.3 %shard_map.109 = bf16[2,8,16,1024]{3,2,1,0:T(8,128)(2,1)S(1)} custom-call(bf16[4,32,1664]{2,1,0:T(8,128)(2,1)S(1)} %bitcast.18, f32[1664]{0:T(1024)S(1)} %copy-done.3, f32[1664]{0:T(1024)S(1)} %copy-done.4, f32[104,3]{1,0:T(8,128)S(1)} %copy.21.turns_ref, f32[4,512]{1,0:T(4,128)S(1)} %maximum_maximum_fusion.lanes_ref, f32[512,2]{1,0:T(8,128)S(1)} %copy.22.columns_ref, ...), custom_call_target="tpu_custom_call" | custom-call | tf_op jit(solution)/shard_map/pallas_call | solution.py:566
  93.5 0.9 copy.23
  (9 shorter events, 0.1 us)
Async XLA Ops:
  5.0 1.5 %copy-start = (bf16[1664,512]{1,0:T(8,128)(2,1)S(1)}, bf16[1664,512]{1,0:T(8,128)(2,1)}, u32[]{:S(2)}) copy-start(bf16[1664,512]{1,0:T(8,128)(2,1)} %merge_hbm.1) | copy-start | bytes 5111812
  6.5 1.3 %copy-start.1 = (bf16[416,1664]{1,0:T(8,128)(2,1)S(1)}, bf16[416,1664]{1,0:T(8,128)(2,1)}, u32[]{:S(2)}) copy-start(bf16[416,1664]{1,0:T(8,128)(2,1)} %out_hbm.1) | copy-start | bytes 4153348
  7.8 1.0 %copy-start.2 = (bf16[128,1664]{1,0:T(8,128)(2,1)S(1)}, bf16[128,1664]{1,0:T(8,128)(2,1)}, u32[]{:S(2)}) copy-start(bf16[128,1664]{1,0:T(8,128)(2,1)} %param.11) | copy-start | bytes 1277956
  8.8 0.7 copy-start.3
  9.5 0.7 copy-start.4
